TPU v7x, 32 devices: a whole 2x2x4 slice. The times are simulated.
32 devices in a mesh: batch: 16 (over z, x, core), mp: 2 (over y).
Axes of the slice: x: 2, y: 2, z: 4, core: 2. Of those that a mesh axis runs over, the one named last changes fastest.
Arguments:
- hidden_in: bfloat16 [18432, 768], P('batch'), may hold values from -6 to 6
- cotangent: bfloat16 [18432, 768], P('batch'), may hold values from -6 to 6
- valid: int32 [64], P('batch'), may hold values from 0 to 1, as said below
- answers: int32 [64, 2], P('batch'), may hold values from 0 to 287, as said below
- query_embed: float32 [8, 128], replicated, may hold values from -1 to 1
- w_qkv: bfloat16 [3, 768, 768], P(None, None, 'mp'), may hold values from -0.21875 to 0.21875
- b_qv: float32 [2, 768], P(None, 'mp'), may hold values from -3 to 3
- w_out: bfloat16 [768, 768], P('mp'), may hold values from -0.875 to 0.875
- b_out: float32 [768], replicated, may hold values from -2 to 2
- gain_attn: float32 [768], replicated, may hold values from 0.5 to 1.5
- shift_attn: float32 [768], replicated, may hold values from -2 to 2
- w_in: bfloat16 [768, 3072], P(None, 'mp'), may hold values from -0.21875 to 0.21875
- b_in: float32 [3072], P('mp'), may hold values from -3 to 3
- w_down: bfloat16 [3072, 768], P('mp'), may hold values from -0.109375 to 0.109375
- b_down: float32 [768], replicated, may hold values from -2 to 2
- gain_ffn: float32 [768], replicated, may hold values from 0.5 to 1.5
- shift_ffn: float32 [768], replicated, may hold values from -2 to 2
- w_ret: float32 [768, 128], replicated, may hold values from -0.21875 to 0.21875
- w_span: float32 [768, 2], replicated, may hold values from -0.21875 to 0.21875
Outputs:
- mll: float32 [8], replicated
- layer_out: bfloat16 [18432, 768], P('batch')
- grad_in: float32 [18432, 768], P('batch')
- grad_w_qkv: float32 [3, 768, 768], P(None, 'batch', 'mp')
- grad_b_qv: float32 [2, 768], P(None, ('mp', 'batch'))
- grad_w_out: float32 [768, 768], P('mp', 'batch')
- grad_b_out: float32 [768], P('batch')
- grad_gain_attn: float32 [768], P('batch')
- grad_shift_attn: float32 [768], P('batch')
- grad_w_in: float32 [768, 3072], P('batch', 'mp')
- grad_b_in: float32 [3072], P(('mp', 'batch'))
- grad_w_down: float32 [3072, 768], P('mp', 'batch')
- grad_b_down: float32 [768], P('batch')
- grad_gain_ffn: float32 [768], P('batch')
- grad_shift_ffn: float32 [768], P('batch')
- grad_w_ret: float32 [768, 128], P('batch')
- grad_w_span: float32 [768, 2], P('batch')
Inputs may be any that keep to these rules, and one draw needn't show every extreme that they name: `valid`: each query's 8 entries hold 4 to 8 ones; some query has exactly 4 and some has 8. `answers`: in each slot start <= end <= start + 8; some slot starts at 0 and some ends at 287.
All inputs are finite; a program needn't handle non-finite values.
Results may differ from a plain program's by a relative error of at most 0.013.
The roundings to bfloat16 on the way count: a program that leaves them out, or rounds other values in their place, can miss the bound.
Values sent between devices are 32-bit elements; how exact they have to be, the bound alone decides.
No kernel may reach another device: no remote copies, remote signals or barrier semaphores. Data moves between devices by JAX's collectives and lax.ppermute only.
A program may use at most 192 MiB of HBM per device.

v0:
```python
import jax
import jax.numpy as jnp
from jax import lax
from jax.sharding import PartitionSpec as P

HEAD_DIM = 64
SEQ = 288
SLOTS = 8


eps = 1e-05
floor_value = -1e30


def merged_2(x, axis, combine):
    everything = jax.tree.map(lambda part: lax.all_gather(part, axis), x)
    initial = jax.tree.map(lambda part: part[0], everything)

    def turn(k, so_far):
        return combine(so_far, jax.tree.map(lambda part: part[k], everything))

    return lax.fori_loop(1, lax.axis_size(axis), turn, initial)


def layer_norm(v, gain, shift):
    centre = v - jnp.mean(v, -1, keepdims=True)
    inverse = lax.rsqrt(jnp.mean(centre * centre, -1, keepdims=True) + eps)
    normed = centre * inverse
    return (normed * gain + shift, normed, inverse)


def norm_back(grad, normed, inverse, gain):
    grad_gain = jnp.sum(grad * normed, 0)
    grad_shift = jnp.sum(grad, 0)
    scaled = grad * gain
    grad_input = inverse * (
        scaled
        - jnp.mean(scaled, -1, keepdims=True)
        - normed * jnp.mean(scaled * normed, -1, keepdims=True)
    )
    return (grad_input, grad_gain, grad_shift)


def forward(hidden_in, weights):
    (
        w_qkv,
        b_qv,
        w_out,
        b_out,
        gain_attn,
        shift_attn,
        w_in,
        b_in,
        w_down,
        b_down,
        gain_ffn,
        shift_ffn,
    ) = weights
    rows = hidden_in.shape[0]
    slots = rows // SEQ
    local = w_qkv.shape[2]
    heads = local // HEAD_DIM
    shape4 = (slots, SEQ, heads, HEAD_DIM)
    proj = jnp.einsum("rd,cde->cre", hidden_in, w_qkv, preferred_element_type=jnp.float32)
    query = (proj[0] + b_qv[0]).astype(jnp.bfloat16)
    keys = proj[1].astype(jnp.bfloat16)
    values = (proj[2] + b_qv[1]).astype(jnp.bfloat16)
    scores = jnp.einsum(
        "bqhd,bkhd->bhqk",
        query.reshape(shape4),
        keys.reshape(shape4),
        preferred_element_type=jnp.float32,
    ) * HEAD_DIM ** (-0.5)
    log_total = jax.nn.logsumexp(scores, axis=-1, keepdims=True)
    probs = jnp.exp(scores - log_total).astype(jnp.bfloat16)
    context = jnp.einsum(
        "bhqk,bkhd->bqhd", probs, values.reshape(shape4), preferred_element_type=jnp.float32
    )
    context = context.reshape(rows, local).astype(jnp.bfloat16)
    attn_part = jnp.dot(context, w_out, preferred_element_type=jnp.float32)
    attended = lax.psum(attn_part, "mp")
    mixed = hidden_in.astype(jnp.float32) + attended + b_out
    first, normed_a, inverse_a = layer_norm(mixed, gain_attn, shift_attn)
    first_low = first.astype(jnp.bfloat16)
    inner = jnp.dot(first_low, w_in, preferred_element_type=jnp.float32) + b_in
    act_low = jax.nn.gelu(inner, approximate=False).astype(jnp.bfloat16)
    ffn_part = jnp.dot(act_low, w_down, preferred_element_type=jnp.float32)
    ffn_out = lax.psum(ffn_part, "mp")
    second, normed_f, inverse_f = layer_norm(first + ffn_out + b_down, gain_ffn, shift_ffn)
    saved = (
        query,
        keys,
        values,
        log_total,
        context,
        first_low,
        normed_a,
        inverse_a,
        inner,
        act_low,
        normed_f,
        inverse_f,
    )
    return (second, saved)


def combine(left, right):
    merged = []
    for pos in (0, 2):
        peak = jnp.maximum(left[pos], right[pos])
        total = left[pos + 1] * jnp.exp(left[pos] - peak) + right[pos + 1] * jnp.exp(
            right[pos] - peak
        )
        merged = merged + [peak, total]
    return tuple(merged)


def query_stats(values_in, member):
    table = jnp.where(member, values_in[:, None], floor_value)
    peak = jnp.max(table, 0)
    total = jnp.sum(jnp.where(member, jnp.exp(table - peak[None, :]), 0.0), 0)
    return (peak, total)


def on_device(
    hidden_in,
    cotangent,
    valid,
    answers,
    query_embed,
    w_qkv,
    b_qv,
    w_out,
    b_out,
    gain_attn,
    shift_attn,
    w_in,
    b_in,
    w_down,
    b_down,
    gain_ffn,
    shift_ffn,
    w_ret,
    w_span,
):
    highest = lax.Precision.HIGHEST
    weights = (
        w_qkv,
        b_qv,
        w_out,
        b_out,
        gain_attn,
        shift_attn,
        w_in,
        b_in,
        w_down,
        b_down,
        gain_ffn,
        shift_ffn,
    )
    rows, width = hidden_in.shape
    slots = rows // SEQ
    second, saved_first = forward(hidden_in, weights)
    base = lax.axis_index("batch") * slots
    owner = (base + jnp.arange(slots)) // SLOTS
    pick = (owner[:, None] == jnp.arange(query_embed.shape[0])[None, :]).astype(jnp.float32)
    lead = second.reshape(slots, SEQ, width)[:, 0, :]
    q_rows = jnp.dot(pick, query_embed, precision=highest)
    embed = jnp.dot(lead, w_ret, precision=highest)
    retrieval = jnp.sum(embed * q_rows, -1)
    logits = jnp.dot(second, w_span, precision=highest).reshape(slots, SEQ, 2)
    log_probs = jax.nn.log_softmax(logits, axis=1)
    marks = (jnp.arange(SEQ)[None, :, None] == answers[:, None, :]).astype(jnp.float32)
    span = jnp.sum(log_probs * marks, axis=(1, 2))
    live = valid > 0
    member = (pick > 0) & live[:, None]
    peak_joint, total_joint = query_stats(retrieval + span, member)
    peak_prior, total_prior = query_stats(retrieval, member)
    stats = merged_2((peak_joint, total_joint, peak_prior, total_prior), "batch", combine)
    lse_joint = stats[0] + jnp.log(stats[1])
    lse_prior = stats[2] + jnp.log(stats[3])
    mll = lse_joint - lse_prior
    slot_joint = jnp.sum(pick * lse_joint[None, :], 1)
    slot_prior = jnp.sum(pick * lse_prior[None, :], 1)
    post = jnp.where(live, jnp.exp(retrieval + span - slot_joint), 0.0)
    prior_weight = jnp.where(live, jnp.exp(retrieval - slot_prior), 0.0)
    d_retrieval = prior_weight - post
    d_logits = (-post)[:, None, None] * (marks - jnp.exp(log_probs))
    d_logits = d_logits.reshape(rows, 2)
    d_embed = d_retrieval[:, None] * q_rows
    d_second = cotangent.astype(jnp.float32) + jnp.dot(d_logits, w_span.T, precision=highest)
    d_second = (
        d_second.reshape(slots, SEQ, width)
        .at[:, 0, :]
        .add(jnp.dot(d_embed, w_ret.T, precision=highest))
        .reshape(rows, width)
    )
    grad_w_span = jnp.dot(second.T, d_logits, precision=highest)
    grad_w_ret = jnp.dot(lead.T, d_embed, precision=highest)
    saved = forward(hidden_in, weights)[1]
    (
        query,
        keys,
        values,
        log_total,
        context,
        first_low,
        normed_a,
        inverse_a,
        inner,
        act_low,
        normed_f,
        inverse_f,
    ) = saved
    d_sum, grad_gain_ffn, grad_shift_ffn = norm_back(d_second, normed_f, inverse_f, gain_ffn)
    grad_b_down = jnp.sum(d_sum, 0)
    d_ffn = d_sum.astype(jnp.bfloat16)
    grad_w_down = jnp.einsum("rf,rd->fd", act_low, d_ffn, preferred_element_type=jnp.float32)
    d_act = jnp.einsum("rd,fd->rf", d_ffn, w_down, preferred_element_type=jnp.float32)
    gelu_value, gelu_back = jax.vjp(lambda v: jax.nn.gelu(v, approximate=False), inner)
    d_inner = gelu_back(d_act)[0].astype(jnp.bfloat16)
    grad_b_in = jnp.sum(d_inner.astype(jnp.float32), 0)
    grad_w_in = jnp.einsum("rd,rf->df", first_low, d_inner, preferred_element_type=jnp.float32)
    d_first_part = jnp.einsum("rf,df->rd", d_inner, w_in, preferred_element_type=jnp.float32)
    d_first = d_sum + lax.psum(d_first_part, "mp")
    d_mixed, grad_gain_attn, grad_shift_attn = norm_back(d_first, normed_a, inverse_a, gain_attn)
    grad_b_out = jnp.sum(d_mixed, 0)
    d_att = d_mixed.astype(jnp.bfloat16)
    grad_w_out = jnp.einsum("rc,rd->cd", context, d_att, preferred_element_type=jnp.float32)
    d_context = jnp.einsum("rd,cd->rc", d_att, w_out, preferred_element_type=jnp.float32).astype(
        jnp.bfloat16
    )
    local = w_qkv.shape[2]
    heads = local // HEAD_DIM
    shape4 = (slots, SEQ, heads, HEAD_DIM)
    query4 = query.reshape(shape4)
    keys4 = keys.reshape(shape4)
    values4 = values.reshape(shape4)
    scale_factor = HEAD_DIM ** (-0.5)
    scores = (
        jnp.einsum("bqhd,bkhd->bhqk", query4, keys4, preferred_element_type=jnp.float32)
        * scale_factor
    )
    probs = jnp.exp(scores - log_total)
    d_context4 = d_context.reshape(shape4)
    d_values = jnp.einsum(
        "bhqk,bqhd->bkhd",
        probs.astype(jnp.bfloat16),
        d_context4,
        preferred_element_type=jnp.float32,
    )
    d_probs = jnp.einsum("bqhd,bkhd->bhqk", d_context4, values4, preferred_element_type=jnp.float32)
    centre = jnp.sum(d_probs * probs, -1, keepdims=True)
    d_scores = (probs * (d_probs - centre) * scale_factor).astype(jnp.bfloat16)
    d_query = jnp.einsum("bhqk,bkhd->bqhd", d_scores, keys4, preferred_element_type=jnp.float32)
    d_keys = jnp.einsum("bhqk,bqhd->bkhd", d_scores, query4, preferred_element_type=jnp.float32)
    d_query = d_query.reshape(rows, local).astype(jnp.bfloat16)
    d_keys = d_keys.reshape(rows, local).astype(jnp.bfloat16)
    d_values = d_values.reshape(rows, local).astype(jnp.bfloat16)
    d_proj = jnp.stack([d_query, d_keys, d_values])
    grad_b_qv = jnp.stack(
        [jnp.sum(d_query.astype(jnp.float32), 0), jnp.sum(d_values.astype(jnp.float32), 0)]
    )
    grad_w_qkv = jnp.einsum("rd,cre->cde", hidden_in, d_proj, preferred_element_type=jnp.float32)
    d_in_part = jnp.einsum("cre,cde->rd", d_proj, w_qkv, preferred_element_type=jnp.float32)
    grad_in = d_mixed + lax.psum(d_in_part, "mp")
    every = (
        lax.psum_scatter(grad_w_qkv, "batch", scatter_dimension=1, tiled=True),
        lax.psum_scatter(grad_b_qv, "batch", scatter_dimension=1, tiled=True),
        lax.psum_scatter(grad_w_out, "batch", scatter_dimension=1, tiled=True),
        lax.psum_scatter(grad_b_out, "batch", scatter_dimension=0, tiled=True),
        lax.psum_scatter(grad_gain_attn, "batch", scatter_dimension=0, tiled=True),
        lax.psum_scatter(grad_shift_attn, "batch", scatter_dimension=0, tiled=True),
        lax.psum_scatter(grad_w_in, "batch", scatter_dimension=0, tiled=True),
        lax.psum_scatter(grad_b_in, "batch", scatter_dimension=0, tiled=True),
        lax.psum_scatter(grad_w_down, "batch", scatter_dimension=1, tiled=True),
        lax.psum_scatter(grad_b_down, "batch", scatter_dimension=0, tiled=True),
        lax.psum_scatter(grad_gain_ffn, "batch", scatter_dimension=0, tiled=True),
        lax.psum_scatter(grad_shift_ffn, "batch", scatter_dimension=0, tiled=True),
        lax.psum_scatter(grad_w_ret, "batch", scatter_dimension=0, tiled=True),
        lax.psum_scatter(grad_w_span, "batch", scatter_dimension=0, tiled=True),
    )
    return (
        mll,
        second.astype(jnp.bfloat16),
        grad_in,
        every[0],
        every[1],
        every[2],
        every[3],
        every[4],
        every[5],
        every[6],
        every[7],
        every[8],
        every[9],
        every[10],
        every[11],
        every[12],
        every[13],
    )


def solution(mesh):
    return jax.shard_map(
        on_device,
        mesh=mesh,
        in_specs=(
            P("batch", None),
            P("batch", None),
            P("batch"),
            P("batch", None),
            P(),
            P(None, None, "mp"),
            P(None, "mp"),
            P("mp", None),
            P(),
            P(),
            P(),
            P(None, "mp"),
            P("mp"),
            P("mp", None),
            P(),
            P(),
            P(),
            P(),
            P(),
        ),
        out_specs=(
            P(),
            P("batch", None),
            P("batch", None),
            P(None, "batch", "mp"),
            P(None, ("mp", "batch")),
            P("mp", "batch"),
            P("batch"),
            P("batch"),
            P("batch"),
            P("batch", "mp"),
            P(("mp", "batch")),
            P("mp", "batch"),
            P("batch"),
            P("batch"),
            P("batch"),
            P("batch", None),
            P("batch", None),
        ),
        check_vma=False,
    )
```

profile of v0, /device:TPU:0, one launch (start us, length us, event | category | flops | bytes accessed | tf_op | source)
XLA Modules:
  0.0 1058.3 jit_solution(18287219291970101323)
XLA Ops:
  7.2 4.7 convolution_bitcast_fusion
  15.0 3.9 squeeze.66
  21.8 3.6 multiply_reduce_fusion.1
  29.6 3.8 squeeze.65
  33.5 6.9 fusion.48
  44.6 4.3 fusion.122
  49.0 97.1 %all-reduce.21.cloned.1.call-done = f32[1152,768]{1,0:T(8,128)} async-done(((f32[1152,768]{1,0:T(8,128)}), f32[1152,768]{1,0:T(8,128)}) %all-reduce.21.cloned.1.call-update) | async-done | bytes 3538960 | tf_op jit(solution)/shard_map/psum | solution.py:81
  146.2 3.1 fusion.117
  150.1 19.4 %multiply_convert_fusion.1 = (bf16[1152,1536]{1,0:T(8,128)(2,1)S(1)}, f32[1152,1536]{1,0:T(8,128)}, f32[1152,1536]{1,0:T(8,128)}) fusion(f32[1536]{0:T(1024)S(1)} %copy-done.54, bf16[768,1536]{1,0:T(8,128)(2,1)S(1)} %copy-done, f32[1152,768]{1,0:T(8,128)S(1)} %get-tuple-element.393, f32[768]{0:T(1024)S(1)} %copy-done.23, f32[768]{0:T(1024)S(1)} %copy-done.20, ...), kind=kOutput, calls=%fused_computation.27 | convolution fusion | flops 2839117824 | bytes 23614464 | tf_op jit(solution)/shard_map/dot_general | solution.py:85
  171.3 4.7 fusion.123
  178.4 92.1 %all-reduce.23.cloned.1.call-done = f32[1152,768]{1,0:T(8,128)} async-done(((f32[1152,768]{1,0:T(8,128)}), f32[1152,768]{1,0:T(8,128)}) %all-reduce.23.cloned.1.call-update) | async-done | bytes 3538960 | tf_op jit(solution)/shard_map/psum | solution.py:88
  270.5 4.2 fusion.115
  279.2 3.1 fusion.124
  285.5 33.5 %all-reduce.14 = (f32[128]{0:T(128)S(1)}, f32[128]{0:T(128)S(1)}, f32[128]{0:T(128)S(1)}, f32[128]{0:T(128)S(1)}) all-reduce(f32[128]{0:T(128)S(1)} %dynamic-update-slice.3, f32[128]{0:T(128)S(1)} %dynamic-update-slice.4, f32[128]{0:T(128)S(1)} %dynamic-update-slice.5, ...), channel_id=2, replica_groups=mesh['batch'=16,'mp'=2] {'batch'}, use_global_device_ids=true, to_apply=%add | all-reduce | flops 512 | bytes 4096
  321.0 4.5 convolution_add_fusion.1
  329.6 3.2 fusion.107
  332.8 3.7 fusion.36
  336.6 4.4 fusion.110
  341.1 10.1 convert_reduce_fusion
  352.9 4.7 fusion.125
  357.9 8.9 fusion.103
  367.0 81.6 %all-reduce.25.cloned.1.call-done = f32[1152,768]{1,0:T(8,128)} async-done(((f32[1152,768]{1,0:T(8,128)}), f32[1152,768]{1,0:T(8,128)}) %all-reduce.25.cloned.1.call-update) | async-done | bytes 3538960 | tf_op jit(solution)/shard_map/psum | solution.py:225
  448.5 6.4 multiply_reduce_fusion.2
  462.5 3.1 copy.107
  465.6 8.0 convert_reduce_fusion.1
  473.6 5.8 fusion.69
  479.4 20.7 %convert_reduce_fusion.2 = (f32[6,64]{1,0:T(8,128)}, bf16[4,6,64,288]{3,2,1,0:T(8,128)(2,1)}) fusion(f32[4,6,288,288]{2,3,1,0:T(8,128)} %fusion.69, f32[4,6,288,288]{2,3,1,0:T(8,128)} %copy-done.1, f32[4,6,288]{2,1,0:T(8,128)} %copy-done.19, bf16[4,288,6,64]{1,0,3,2:T(4,128)(2,1)} %copy-done.14), kind=kOutput, calls=%fused_computation.76 | convolution fusion | flops 274053792 | bytes 17723904 | tf_op jit(solution)/shard_map/bhqk,bkhd->bqhd/dot_general | solution.py:255
  500.1 20.1 %fusion.49 = bf16[4,288,6,64]{1,3,2,0:T(8,128)(2,1)} fusion(f32[4,6,288,288]{2,3,1,0:T(8,128)} %fusion.69, f32[4,6,288,288]{2,3,1,0:T(8,128)} %copy-done.1, f32[4,6,288]{2,1,0:T(8,128)} %copy-done.19, f32[4,288,6,64]{1,0,3,2:T(4,128)} %squeeze.66, f32[6,64]{1,0:T(8,128)} %copy-done.30), kind=kOutput, calls=%fused_computation.86 | convolution fusion | flops 274054176 | bytes 18608640 | tf_op jit(solution)/shard_map/bhqk,bqhd->bkhd/dot_general | solution.py:256
  520.2 3.2 copy.130
  523.4 3.4 reshape.313
  526.8 3.9 copy.129
  530.7 4.1 reshape.312
  534.8 3.9 copy.128
  538.7 4.1 reshape.311
  547.2 4.4 convolution_bitcast_fusion.2
  551.6 6.3 copy.120
  557.9 6.6 convolution_bitcast_fusion.1
  566.9 4.3 fusion.58
  571.5 9.0 fusion.104
  580.5 8.6 fusion.61
  592.8 61.8 %all-reduce.13 = (f32[2,384]{1,0:T(2,128)S(1)}, f32[768]{0:T(1024)S(1)}, f32[768]{0:T(1024)S(1)}, f32[768]{0:T(1024)S(1)}, f32[1536]{0:T(1024)S(1)}, /*index=5*/...) all-reduce(f32[2,384]{1,0:T(2,128)S(1)} %pad_maximum_fusion, ...), channel_id=7, replica_groups=mesh['batch'=16,'mp'=2] {'batch'}, use_global_device_ids=true, to_apply=%region_31.32.clone | all-reduce | flops 6912 | bytes 55296
  659.3 16.2 %all-reduce.29.cloned.1.call-done = f32[3,768,384]{2,0,1:T(4,128)} async-done(((f32[3,768,384]{2,0,1:T(4,128)}), f32[3,768,384]{2,0,1:T(4,128)}) %all-reduce.29.cloned.1.call-update) | async-done | bytes 3538960
  677.2 94.4 %all-reduce.27.cloned.1.call-done = f32[1152,768]{1,0:T(8,128)} async-done(((f32[1152,768]{1,0:T(8,128)}), f32[1152,768]{1,0:T(8,128)}) %all-reduce.27.cloned.1.call-update) | async-done | bytes 3538960 | tf_op jit(solution)/shard_map/psum | solution.py:266
  771.5 5.3 add.289
  776.9 54.7 %reduce-scatter.15.cloned.1.call-done = f32[48,128]{1,0:T(8,128)} async-done(((f32[768,128]{1,0:T(8,128)}), f32[48,128]{1,0:T(8,128)}) %reduce-scatter.15.cloned.1.call-update) | async-done | bytes 24592 | tf_op jit(solution)/shard_map/reduce_scatter | solution.py:280
  831.6 61.4 %reduce-scatter.9.cloned.1.call-done = f32[384,48]{0,1:T(8,128)} async-done(((f32[384,768]{0,1:T(8,128)}), f32[384,48]{0,1:T(8,128)}) %reduce-scatter.9.cloned.1.call-update) | async-done | bytes 73744 | tf_op jit(solution)/shard_map/reduce_scatter | solution.py:270
  892.9 79.0 %reduce-scatter.11.cloned.1.call-done = f32[48,1536]{1,0:T(8,128)} async-done(((f32[768,1536]{1,0:T(8,128)}), f32[48,1536]{1,0:T(8,128)}) %reduce-scatter.11.cloned.1.call-update) | async-done | bytes 294928 | tf_op jit(solution)/shard_map/reduce_scatter | solution.py:274
  971.9 79.4 %reduce-scatter.13.cloned.1.call-done = f32[1536,48]{0,1:T(8,128)} async-done(((f32[1536,768]{0,1:T(8,128)}), f32[1536,48]{0,1:T(8,128)}) %reduce-scatter.13.cloned.1.call-update) | async-done | bytes 294928 | tf_op jit(solution)/shard_map/reduce_scatter | solution.py:276
  (237 shorter events, 57.6 us)
Async XLA Ops:
  7.2 142.7 %copy-start = (bf16[768,1536]{1,0:T(8,128)(2,1)S(1)}, bf16[768,1536]{1,0:T(8,128)(2,1)}, u32[]{:S(2)}) copy-start(bf16[768,1536]{1,0:T(8,128)(2,1)} %param.34) | copy-start | bytes 7077892
  7.2 139.0 %all-reduce.21.cloned.1.call-start = ((), (), s32[]{:S(2)}) async-start(), calls=%async_computation.5 | async-start | bytes 7077888 | tf_op jit(solution)/shard_map/psum | solution.py:81
  15.0 6.7 copy-start.48
  21.7 3.8 copy-start.14
  21.8 3.7 copy-start.30
  25.5 4.1 copy-start.1
  29.5 10.8 %copy-start.19 = (f32[4,6,288]{2,1,0:T(8,128)}, f32[4,6,288]{2,1,0:T(8,128)S(1)}, u32[]{:S(2)}) copy-start(f32[4,6,288]{2,1,0:T(8,128)S(1)} %log_add_fusion) | copy-start | bytes 82948
  33.5 6.9 copy-start.28
  44.6 4.3 copy-start.11
  48.9 97.2 %copy-start.46 = (f32[768]{0:T(1024)S(1)}, f32[768]{0:T(1024)}, u32[]{:S(2)}) copy-start(f32[768]{0:T(1024)} %param.31) | copy-start | bytes 9220
  49.0 221.6 %all-reduce.23.cloned.1.call-start = ((), (), s32[]{:S(2)}) async-start(), calls=%async_computation.6 | async-start | bytes 7077888 | tf_op jit(solution)/shard_map/psum | solution.py:88
  149.3 20.2 %copy-start.2 = (f32[1152,768]{1,0:T(8,128)}, f32[1152,768]{1,0:T(8,128)S(1)}, u32[]{:S(2)}) copy-start(f32[1152,768]{1,0:T(8,128)S(1)} %get-tuple-element.393) | copy-start | bytes 10616836
  150.1 21.2 %copy-start.52 = (bf16[1536,768]{1,0:T(8,128)(2,1)S(1)}, bf16[1536,768]{1,0:T(8,128)(2,1)}, u32[]{:S(2)}) copy-start(bf16[1536,768]{1,0:T(8,128)(2,1)} %param.36) | copy-start | bytes 7077892
  176.0 94.5 %copy-start.44 = (f32[768]{0:T(1024)S(1)}, f32[768]{0:T(1024)}, u32[]{:S(2)}) copy-start(f32[768]{0:T(1024)} %param.37) | copy-start | bytes 9220
  176.0 272.5 %all-reduce.25.cloned.1.call-start = ((), (), s32[]{:S(2)}) async-start(), calls=%async_computation.7 | async-start | bytes 7077888 | tf_op jit(solution)/shard_map/psum | solution.py:225
  178.4 149.1 %copy-start.32 = (f32[4,128]{1,0:T(4,128)}, f32[4,128]{1,0:T(4,128)S(1)}, u32[]{:S(2)}) copy-start(f32[4,128]{1,0:T(4,128)S(1)} %fusion.87) | copy-start | bytes 6148
  274.8 2.6 copy-start.4
  275.5 3.7 copy-start.31
  277.4 6.6 copy-start.18
  283.9 48.9 %copy-start.25 = (f32[4,1,768]{2,1,0:T(1,128)}, f32[4,1,768]{2,1,0:T(1,128)S(1)}, u32[]{:S(2)}) copy-start(f32[4,1,768]{2,1,0:T(1,128)S(1)} %slice.76) | copy-start | bytes 36868
  320.9 11.9 %copy-start.42 = (f32[4]{0:T(128)}, f32[4]{0:T(128)S(1)}, u32[]{:S(2)}) copy-start(f32[4]{0:T(128)S(1)} %get-tuple-element.398) | copy-start | bytes 52
  329.6 3.2 copy-start.5
  336.6 4.4 copy-start.53
  341.0 10.1 copy-start.10
  357.7 233.4 %reduce-scatter.17.cloned.1.call-start = ((), (), s32[]{:S(2)}) async-start(), calls=%async_computation.13 | async-start | bytes 417792
  366.9 308.6 %all-reduce.29.cloned.1.call-start = ((), (), s32[]{:S(2)}) async-start(), calls=%async_computation.14 | async-start | bytes 9437184
  448.5 6.4 copy-start.3
  454.9 3.8 copy-start.16
  465.6 8.0 copy-start.9
  465.6 8.0 copy-start.29
  500.1 20.1 %copy-start.13 = (bf16[4,6,64,288]{3,2,1,0:T(8,128)(2,1)S(1)}, bf16[4,6,64,288]{3,2,1,0:T(8,128)(2,1)}, u32[]{:S(2)}) copy-start(bf16[4,6,64,288]{3,2,1,0:T(8,128)(2,1)} %get-tuple-element.406) | copy-start | bytes 2654212
  542.8 4.4 copy-start.17
  557.9 213.7 %all-reduce.27.cloned.1.call-start = ((), (), s32[]{:S(2)}) async-start(), calls=%async_computation.8 | async-start | bytes 7077888 | tf_op jit(solution)/shard_map/psum | solution.py:266
  564.6 267.0 %reduce-scatter.15.cloned.1.call-start = ((), (), s32[]{:S(2)}) async-start(), calls=%async_computation.12 | async-start | bytes 417792 | tf_op jit(solution)/shard_map/reduce_scatter | solution.py:280
  566.8 4.6 copy-start.21
  566.9 4.6 copy-start.24
  566.9 326.1 %reduce-scatter.9.cloned.1.call-start = ((), (), s32[]{:S(2)}) async-start(), calls=%async_computation.9 | async-start | bytes 1253376 | tf_op jit(solution)/shard_map/reduce_scatter | solution.py:270
  571.3 400.7 %reduce-scatter.11.cloned.1.call-start = ((), (), s32[]{:S(2)}) async-start(), calls=%async_computation.10 | async-start | bytes 5013504 | tf_op jit(solution)/shard_map/reduce_scatter | solution.py:274
  580.5 470.8 %reduce-scatter.13.cloned.1.call-start = ((), (), s32[]{:S(2)}) async-start(), calls=%async_computation.11 | async-start | bytes 5013504 | tf_op jit(solution)/shard_map/reduce_scatter | solution.py:276
  589.1 3.4 copy-start.39
  589.1 3.5 copy-start.47
  589.1 3.6 copy-start.34
  589.1 3.6 copy-start.35
  589.1 3.6 copy-start.36
  589.1 3.6 copy-start.37
  589.1 3.6 copy-start.38
  589.1 3.6 copy-start.40
  589.1 3.6 copy-start.41
  (19 other events, 24.8 us)
Sparse Core Ops, SparseCore 0:
  49.1 97.0 all-reduce.20
  176.1 94.3 all-reduce.22
  357.8 90.6 all-reduce.24
  452.3 55.5 reduce-scatter.16
  558.0 117.4 all-reduce.28
  677.6 93.8 all-reduce.26
  776.0 55.5 reduce-scatter.14
  835.8 57.1 reduce-scatter.8
  897.4 74.5 reduce-scatter.10
  976.7 74.5 reduce-scatter.12
where the time goes:
time: 1060 us
  waiting for transfers between devices  656 us (62%)
  matrix products  166 us (16%)
  blocking collectives  95.4 us (9%)
  local copies, waits for them, and re-layouts  83.1 us (8%)
  other arithmetic  39.1 us (4%)
  between operations  17.6 us (2%)
    psum x1, waiting for transfers between devices, forward(): attended = lax.psum(attn_part, 'mp')  97.1 us
    unnamed x2, blocking collectives  95.4 us
    psum x1, waiting for transfers between devices, on_device(): grad_in = d_mixed + lax.psum(d_in_part, 'mp')  94.4 us
    psum x1, waiting for transfers between devices, forward(): ffn_out = lax.psum(ffn_part, 'mp')  92.1 us
    psum x1, waiting for transfers between devices, on_device(): d_first = d_sum + lax.psum(d_first_part, 'mp')  81.6 us
    reduce_scatter x1, waiting for transfers between devices, on_device(): lax.psum_scatter(grad_w_down, 'batch', scatter_dimension=1, tiled=True)  79.4 us
    reduce_scatter x1, waiting for transfers between devices, on_device(): lax.psum_scatter(grad_w_in, 'batch', scatter_dimension=0, tiled=True)  79 us
    reduce_scatter x1, waiting for transfers between devices, on_device(): lax.psum_scatter(grad_w_out, 'batch', scatter_dimension=1, tiled=True)  61.4 us
  transfers between devices with their start and end apart: 10, of which 9 were waited for; matrix products, arithmetic and copies ran while one was open for 15% of the time, Pallas kernels for 0%

commit v1 on v0

v1 whole, which is shorter than its diff:
```python
import functools

import jax
import jax.numpy as jnp
from jax import lax
from jax.experimental import pallas as pl
from jax.experimental.pallas import tpu as pltpu
from jax.sharding import PartitionSpec as P

HEAD_DIM = 64
SEQ = 288
SLOTS = 8
BLOCKS = 16
CORE, X, Z0, Z1 = 1, 2, 4, 8
EPS = 1e-05
FLOOR = -1e30
F32 = jnp.float32
BF16 = jnp.bfloat16
HIGHEST = lax.Precision.HIGHEST


def across(v, mask):
    n = lax.axis_size("batch")
    return lax.ppermute(v, "batch", [(i, i ^ mask) for i in range(n)])


def over_y(v):
    return lax.ppermute(v, "mp", [(0, 1), (1, 0)])


def bit_mask(bit):
    return bit * (lax.axis_size("batch") // BLOCKS)


def assemble_kernel(order, me_ref, *refs):
    out_ref = refs[-1]
    rows = out_ref.shape[0] // 8
    piece = 0
    for ref in refs[:-1]:
        for k in range(ref.shape[0] // rows):
            start = pl.multiple_of((order[piece] ^ me_ref[0]) * rows, rows)
            out_ref[pl.ds(start, rows), :] = ref[pl.ds(k * rows, rows), :].astype(BF16)
            piece += 1


def assemble(parts, order, me):
    rows = sum(p.shape[0] for p in parts)
    return pl.pallas_call(
        functools.partial(assemble_kernel, order),
        out_shape=jax.ShapeDtypeStruct((rows, parts[0].shape[1]), BF16),
        in_specs=[pl.BlockSpec(memory_space=pltpu.SMEM)]
        + [pl.BlockSpec(memory_space=pltpu.VMEM)] * len(parts),
        out_specs=pl.BlockSpec(memory_space=pltpu.VMEM),
        compiler_params=pltpu.CompilerParams(vmem_limit_bytes=50 * 2**20),
    )((me & 7).reshape(1), *parts)


def other_half(w, bits, me):
    rows = w.shape[0] // 8
    mine = lax.dynamic_slice_in_dim(w, (me & 7) * rows, rows, 0).astype(F32)
    parts = [over_y(mine)]
    order = [0]
    for bit in bits:
        held = parts[0] if len(parts) == 1 else jnp.concatenate(parts)
        parts = [held, across(held, bit_mask(bit))]
        order = order + [r | bit for r in order]
    return assemble(parts, tuple(order), me)


def place_kernel(y_ref, mine_ref, theirs_ref, out_ref):
    rows = mine_ref.shape[0]
    at = pl.multiple_of(y_ref[0] * rows, rows)
    out_ref[pl.ds(at, rows), :] = mine_ref[...].astype(out_ref.dtype)
    at = pl.multiple_of((1 - y_ref[0]) * rows, rows)
    out_ref[pl.ds(at, rows), :] = theirs_ref[...].astype(out_ref.dtype)


def place(mine, theirs, y, dtype):
    rows, width = mine.shape
    return pl.pallas_call(
        place_kernel,
        out_shape=jax.ShapeDtypeStruct((2 * rows, width), dtype),
        in_specs=[pl.BlockSpec(memory_space=pltpu.SMEM)]
        + [pl.BlockSpec(memory_space=pltpu.VMEM)] * 2,
        out_specs=pl.BlockSpec(memory_space=pltpu.VMEM),
        compiler_params=pltpu.CompilerParams(vmem_limit_bytes=50 * 2**20),
    )(y.reshape(1), mine, theirs)


def row_order(bits):
    order = []
    for p in range(BLOCKS):
        r = 0
        for k, bit in enumerate(bits):
            if (p >> (len(bits) - 1 - k)) & 1:
                r |= bit
        order.append(r)
    return order


def relative_rows(a, bits, me):
    width = a.shape[1]
    t = a.T.reshape(BLOCKS, width // BLOCKS, a.shape[0])
    index = jnp.array(row_order(bits), jnp.int32) ^ me
    return jnp.take(t, index, axis=0).reshape(width, a.shape[0])


def reduce_scatter(own, other, steps):
    for step in steps:
        if step == "y":
            own, other = own + over_y(other), None
        else:
            half = own.shape[0] // 2
            mask = bit_mask(step)
            own = own[:half] + across(own[half:], mask)
            if other is not None:
                other = other[:half] + across(other[half:], mask)
    rest = lax.axis_size("batch") // BLOCKS
    if rest > 1:
        groups = [[g * rest + k for k in range(rest)] for g in range(BLOCKS)]
        own = lax.psum_scatter(
            own, "batch", scatter_dimension=0, axis_index_groups=groups, tiled=True
        )
    return own


def total(v, y_part):
    own, other = y_part
    n = v.shape[0]
    both = jnp.concatenate([v, own]) + over_y(jnp.concatenate([v, other]))
    mask = 1
    while mask < lax.axis_size("batch"):
        both = both + across(both, mask)
        mask *= 2
    return both[:n], both[n:]


def layer_norm(v, gain, shift):
    centre = v - jnp.mean(v, -1, keepdims=True)
    inverse = lax.rsqrt(jnp.mean(centre * centre, -1, keepdims=True) + EPS)
    normed = centre * inverse
    return (normed * gain + shift, normed, inverse)


def norm_back(grad, normed, inverse, gain):
    grad_gain = jnp.sum(grad * normed, 0)
    grad_shift = jnp.sum(grad, 0)
    scaled = grad * gain
    grad_input = inverse * (
        scaled
        - jnp.mean(scaled, -1, keepdims=True)
        - normed * jnp.mean(scaled * normed, -1, keepdims=True)
    )
    return (grad_input, grad_gain, grad_shift)


def attention(x, w, b, w_out):
    rows = x.shape[0]
    slots = rows // SEQ
    local = w.shape[2]
    shape4 = (slots, SEQ, local // HEAD_DIM, HEAD_DIM)
    proj = jnp.einsum("rd,cde->cre", x, w, preferred_element_type=F32)
    q = (proj[0] + b[0]).astype(BF16)
    k = proj[1].astype(BF16)
    v = (proj[2] + b[1]).astype(BF16)
    scores = jnp.einsum(
        "bqhd,bkhd->bhqk", q.reshape(shape4), k.reshape(shape4), preferred_element_type=F32
    ) * HEAD_DIM ** (-0.5)
    lse = jax.nn.logsumexp(scores, axis=-1, keepdims=True)
    probs = jnp.exp(scores - lse).astype(BF16)
    context = jnp.einsum(
        "bhqk,bkhd->bqhd", probs, v.reshape(shape4), preferred_element_type=F32
    )
    context = context.reshape(rows, local).astype(BF16)
    return q, k, v, lse, context, jnp.dot(context, w_out, preferred_element_type=F32)


def attention_back(x, w, q, k, v, lse, d_context, x_rel):
    rows = x.shape[0]
    slots = rows // SEQ
    local = w.shape[2]
    shape4 = (slots, SEQ, local // HEAD_DIM, HEAD_DIM)
    q4, k4, v4, dc4 = (a.reshape(shape4) for a in (q, k, v, d_context))
    scale = HEAD_DIM ** (-0.5)
    scores = jnp.einsum("bqhd,bkhd->bhqk", q4, k4, preferred_element_type=F32) * scale
    probs = jnp.exp(scores - lse)
    d_v = jnp.einsum("bhqk,bqhd->bkhd", probs.astype(BF16), dc4, preferred_element_type=F32)
    d_probs = jnp.einsum("bqhd,bkhd->bhqk", dc4, v4, preferred_element_type=F32)
    centre = jnp.sum(d_probs * probs, -1, keepdims=True)
    d_scores = (probs * (d_probs - centre) * scale).astype(BF16)
    d_q = jnp.einsum("bhqk,bkhd->bqhd", d_scores, k4, preferred_element_type=F32)
    d_k = jnp.einsum("bhqk,bqhd->bkhd", d_scores, q4, preferred_element_type=F32)
    d_q, d_k, d_v = (a.reshape(rows, local).astype(BF16) for a in (d_q, d_k, d_v))
    sums = jnp.concatenate([jnp.sum(d_q.astype(F32), 0), jnp.sum(d_v.astype(F32), 0)])
    grads = [jnp.dot(x_rel, d, preferred_element_type=F32) for d in (d_q, d_k, d_v)]
    part = sum(
        jnp.dot(d, w[c].T, preferred_element_type=F32) for c, d in enumerate((d_q, d_k, d_v))
    )
    return sums, jnp.concatenate(grads, 1), part


def merge(a, b):
    peak = jnp.maximum(a[0], b[0])
    return peak, a[1] * jnp.exp(a[0] - peak) + b[1] * jnp.exp(b[0] - peak)


def on_device(
    hidden_in,
    cotangent,
    valid,
    answers,
    query_embed,
    w_qkv,
    b_qv,
    w_out,
    b_out,
    gain_attn,
    shift_attn,
    w_in,
    b_in,
    w_down,
    b_down,
    gain_ffn,
    shift_ffn,
    w_ret,
    w_span,
):
    here = lax.axis_index("batch")
    y = lax.axis_index("mp")
    me = here // (lax.axis_size("batch") // BLOCKS)
    width = hidden_in.shape[1]
    rows = hidden_in.shape[0] // 2
    slots = rows // SEQ
    slots_here = 2 * slots
    per_query = SLOTS // slots_here
    n_queries = query_embed.shape[0]

    cols = w_qkv.shape[2]
    w_qkv2 = other_half(w_qkv.reshape(-1, cols), (Z0, X, CORE), me).reshape(w_qkv.shape)
    w_out2 = other_half(w_out, (X, Z0, CORE), me)
    w_in2 = other_half(w_in, (Z0, X, CORE), me)
    w_down2 = other_half(w_down, (X, Z0, CORE), me)
    biases = over_y(jnp.concatenate([b_qv.reshape(-1), b_in]))
    b_qv2 = biases[: b_qv.size].reshape(b_qv.shape)
    b_in2 = biases[b_qv.size :]

    x = lax.dynamic_slice_in_dim(hidden_in, y * rows, rows, 0)
    cot = lax.dynamic_slice_in_dim(cotangent, y * rows, rows, 0)
    live = lax.dynamic_slice_in_dim(valid, y * slots, slots, 0) > 0
    marked = lax.dynamic_slice_in_dim(answers, y * slots, slots, 0)

    q1, k1, v1, lse1, ctx1, part1 = attention(x, w_qkv, b_qv, w_out)
    q2, k2, v2, lse2, ctx2, part2 = attention(x, w_qkv2, b_qv2, w_out2)
    mixed = x.astype(F32) + (part1 + part2) + b_out
    first, normed_a, inverse_a = layer_norm(mixed, gain_attn, shift_attn)
    first_low = first.astype(BF16)

    def up(w, b):
        inner = jnp.dot(first_low, w, preferred_element_type=F32) + b
        return inner, jax.nn.gelu(inner, approximate=False).astype(BF16)

    inner1, act1 = up(w_in, b_in)
    inner2, act2 = up(w_in2, b_in2)
    ffn = jnp.dot(act1, w_down, preferred_element_type=F32) + jnp.dot(
        act2, w_down2, preferred_element_type=F32
    )
    second, normed_f, inverse_f = layer_norm(first + ffn + b_down, gain_ffn, shift_ffn)
    layer_out = place(second, over_y(second), y, BF16)

    query = here // per_query
    q_row = lax.dynamic_slice_in_dim(query_embed, query, 1, 0)
    lead = second.reshape(slots, SEQ, width)[:, 0, :]
    embed = jnp.dot(lead, w_ret, precision=HIGHEST)
    retrieval = jnp.sum(embed * q_row, -1)
    logits = jnp.dot(second, w_span, precision=HIGHEST).reshape(slots, SEQ, 2)
    log_probs = jax.nn.log_softmax(logits, axis=1)
    marks = (jnp.arange(SEQ)[None, :, None] == marked[:, None, :]).astype(F32)
    span = jnp.sum(log_probs * marks, axis=(1, 2))
    table = jnp.where(live, jnp.stack([retrieval + span, retrieval]), FLOOR)
    peak = jnp.max(table, 1)
    sums = jnp.sum(jnp.where(live, jnp.exp(table - peak[:, None]), 0.0), 1)
    stats = jnp.stack([peak, sums])
    stats = jnp.stack(merge(stats, over_y(stats)))
    mask = 1
    while mask < per_query:
        stats = jnp.stack(merge(stats, across(stats, mask)))
        mask *= 2
    lse = stats[0] + jnp.log(stats[1])
    mll_mine = jnp.where(
        (jnp.arange(n_queries) == query) & (y == 0) & (here % per_query == 0), lse[0] - lse[1], 0.0
    )
    post = jnp.where(live, jnp.exp(retrieval + span - lse[0]), 0.0)
    prior = jnp.where(live, jnp.exp(retrieval - lse[1]), 0.0)
    d_retrieval = prior - post
    d_logits = (-post)[:, None, None] * (marks - jnp.exp(log_probs))
    d_logits = d_logits.reshape(rows, 2)
    d_embed = d_retrieval[:, None] * q_row
    d_second = cot.astype(F32) + jnp.dot(d_logits, w_span.T, precision=HIGHEST)
    d_second = (
        d_second.reshape(slots, SEQ, width)
        .at[:, 0, :]
        .add(jnp.dot(d_embed, w_ret.T, precision=HIGHEST))
        .reshape(rows, width)
    )
    g_span = jnp.dot(second.T, d_logits, precision=HIGHEST)
    lead_rel = relative_rows(lead, (CORE, X, Z0, Z1), me)
    g_ret = jnp.dot(lead_rel, d_embed, precision=HIGHEST)

    d_sum, g_gain_ffn, g_shift_ffn = norm_back(d_second, normed_f, inverse_f, gain_ffn)
    g_b_down = jnp.sum(d_sum, 0)
    d_ffn = d_sum.astype(BF16)
    down_steps = (CORE, "y", X, Z0, Z1)
    d_ffn_rel = relative_rows(d_ffn, (CORE, X, Z0, Z1), me)
    g_w_down = reduce_scatter(
        jnp.dot(d_ffn_rel, act1, preferred_element_type=F32),
        jnp.dot(d_ffn_rel, act2, preferred_element_type=F32),
        down_steps,
    )

    def down_back(inner, w):
        d_act = jnp.dot(d_ffn, w.T, preferred_element_type=F32)
        return jax.vjp(lambda v: jax.nn.gelu(v, approximate=False), inner)[1](d_act)[0].astype(BF16)

    d_inner1 = down_back(inner1, w_down)
    d_inner2 = down_back(inner2, w_down2)
    g_b_in = (jnp.sum(d_inner1.astype(F32), 0), jnp.sum(d_inner2.astype(F32), 0))
    first_rel = relative_rows(first_low, (CORE, X, Z0, Z1), me)
    g_w_in = reduce_scatter(
        jnp.concatenate([jnp.dot(first_rel, d_inner1, preferred_element_type=F32), g_ret], 1),
        jnp.concatenate([jnp.dot(first_rel, d_inner2, preferred_element_type=F32), g_ret], 1),
        (CORE, X, Z0, Z1, "y"),
    )
    d_first = d_sum + (
        jnp.dot(d_inner1, w_in.T, preferred_element_type=F32)
        + jnp.dot(d_inner2, w_in2.T, preferred_element_type=F32)
    )

    d_mixed, g_gain_attn, g_shift_attn = norm_back(d_first, normed_a, inverse_a, gain_attn)
    g_b_out = jnp.sum(d_mixed, 0)
    d_att = d_mixed.astype(BF16)
    late = (CORE, Z0, X, Z1)
    d_att_rel = relative_rows(d_att, late, me)
    x_rel = relative_rows(x, late, me)
    g_w_out = reduce_scatter(
        jnp.dot(d_att_rel, ctx1, preferred_element_type=F32),
        jnp.dot(d_att_rel, ctx2, preferred_element_type=F32),
        late + ("y",),
    )
    d_ctx1 = jnp.dot(d_att, w_out.T, preferred_element_type=F32).astype(BF16)
    d_ctx2 = jnp.dot(d_att, w_out2.T, preferred_element_type=F32).astype(BF16)
    s1, g1, in1 = attention_back(x, w_qkv, q1, k1, v1, lse1, d_ctx1, x_rel)
    s2, g2, in2 = attention_back(x, w_qkv2, q2, k2, v2, lse2, d_ctx2, x_rel)
    g_w_qkv = reduce_scatter(g1, g2, late + ("y",))
    g_in = d_mixed + (in1 + in2)
    grad_in = place(g_in, over_y(g_in), y, F32)

    common = [g_b_out, g_gain_attn, g_shift_attn, g_b_down, g_gain_ffn, g_shift_ffn]
    common = jnp.concatenate(common + [g_span[:, 0], g_span[:, 1], mll_mine])
    common, own = total(
        common, (jnp.concatenate([s1, g_b_in[0]]), jnp.concatenate([s2, g_b_in[1]]))
    )
    few = width // lax.axis_size("batch")
    vectors = [
        lax.dynamic_slice_in_dim(common, k * width + here * few, few, 0) for k in range(8)
    ]
    mll = common[8 * width :]
    few_q = cols // lax.axis_size("batch")
    few_i = b_in.shape[0] // lax.axis_size("batch")
    g_b_qv = jnp.stack(
        [lax.dynamic_slice_in_dim(own, k * cols + here * few_q, few_q, 0) for k in range(2)]
    )
    g_b_in = lax.dynamic_slice_in_dim(own, 2 * cols + here * few_i, few_i, 0)
    half = w_in.shape[1]
    return (
        mll,
        layer_out,
        grad_in,
        jnp.stack([g_w_qkv[:, c * cols : (c + 1) * cols] for c in range(3)]),
        g_b_qv,
        g_w_out.T,
        vectors[0],
        vectors[1],
        vectors[2],
        g_w_in[:, :half],
        g_b_in,
        g_w_down.T,
        vectors[3],
        vectors[4],
        vectors[5],
        g_w_in[:, half:],
        jnp.stack([vectors[6], vectors[7]], 1),
    )


def solution(mesh):
    return jax.shard_map(
        on_device,
        mesh=mesh,
        in_specs=(
            P("batch", None),
            P("batch", None),
            P("batch"),
            P("batch", None),
            P(),
            P(None, None, "mp"),
            P(None, "mp"),
            P("mp", None),
            P(),
            P(),
            P(),
            P(None, "mp"),
            P("mp"),
            P("mp", None),
            P(),
            P(),
            P(),
            P(),
            P(),
        ),
        out_specs=(
            P(),
            P("batch", None),
            P("batch", None),
            P(None, "batch", "mp"),
            P(None, ("mp", "batch")),
            P("mp", "batch"),
            P("batch"),
            P("batch"),
            P("batch"),
            P("batch", "mp"),
            P(("mp", "batch")),
            P("mp", "batch"),
            P("batch"),
            P("batch"),
            P("batch"),
            P("batch", None),
            P("batch", None),
        ),
        check_vma=False,
    )
```

time: 1060 us -> 677 us (0.64)
  waiting for transfers between devices: 656 us -> 195 us
  blocking collectives: 95.4 us -> 0 us
  local copies, waits for them, and re-layouts: 83.1 us -> 150 us
  starting transfers between devices: 0.76 us -> 46.3 us
  other arithmetic: 39.1 us -> 82.2 us
  Pallas kernels: 0 us -> 14.6 us
  matrix products: 166 us -> 180 us
  between operations: 17.6 us -> 4.11 us
    psum x4 -> x0, waiting for transfers between devices: 365 us -> none  [the longest x1 97.1 us: forward(): attended = lax.psum(attn_part, 'mp')]
    reduce_scatter x4 -> x0, waiting for transfers between devices: 274 us -> none  [the longest x1 79.4 us: on_device(): lax.psum_scatter(grad_w_down, 'batch', scatter_dimension=1, tiled=True)]
    ppermute x0 -> x59, waiting for transfers between devices: none -> 195 us  [the longest x46 165 us: across(): return lax.ppermute(v, 'batch', [(i, i ^ mask) for i in range(n)])]
    unnamed x2 -> x0, blocking collectives: 95.4 us -> none
    ppermute x0 -> x59, starting transfers between devices: none -> 46.3 us  [the longest x46 29.8 us: across(): return lax.ppermute(v, 'batch', [(i, i ^ mask) for i in range(n)])]
    add x18 -> x36, other arithmetic: 5.8 us -> 30.5 us  [the longest x12 12.6 us: reduce_scatter(): other = other[:half] + across(other[half:], mask)]
    dot_general x24 -> x50, matrix products: 157 us -> 180 us  [the longest x2 23.3 us: up(): inner = jnp.dot(first_low, w, preferred_element_type=F32) + b]
    slice x3 -> x45, local copies, waits for them, and re-layouts: 3.06 us -> 22.4 us  [the longest x18 9.39 us: reduce_scatter(): own = own[:half] + across(own[half:], mask)]
  transfers between devices with their start and end apart: 10 -> 59, of which waited for: 9 -> 25; matrix products, arithmetic and copies ran while one was open for 15% -> 30% of each run, Pallas kernels for 0% -> 2%
where the time goes in v1:
time: 677 us; the launch traced here: 672 us
  waiting for transfers between devices  195 us (29%)
  matrix products  180 us (27%)
  local copies, waits for them, and re-layouts  150 us (22%)
  other arithmetic  82.2 us (12%)
  starting transfers between devices  46.3 us (7%)
  Pallas kernels  14.6 us (2%)
    ppermute x46, waiting for transfers between devices, across(): return lax.ppermute(v, 'batch', [(i, i ^ mask) for i in range(n)])  165 us
    unnamed x269, local copies, waits for them, and re-layouts  30.8 us
    ppermute x13, waiting for transfers between devices, over_y(): return lax.ppermute(v, 'mp', [(0, 1), (1, 0)])  30.3 us
    ppermute x46, starting transfers between devices, across(): return lax.ppermute(v, 'batch', [(i, i ^ mask) for i in range(n)])  29.8 us
    convert_element_type x12, local copies, waits for them, and re-layouts, attention_back(): a.reshape(rows, local).astype(BF16)  24.8 us
    dot_general x2, matrix products, up(): inner = jnp.dot(first_low, w, preferred_element_type=F32) + b  23.3 us
    dot_general x2, matrix products, attention_back(): jnp.einsum('bhqk,bkhd->bqhd', d_scores, k4, preferred_element_type=F32)  21.7 us
    dot_general x2, matrix products, attention_back(): jnp.einsum('bhqk,bqhd->bkhd', d_scores, q4, preferred_element_type=F32)  21.3 us
  transfers between devices with their start and end apart: 59, of which 25 were waited for; matrix products, arithmetic and copies ran while one was open for 30% of the time, Pallas kernels for 2%

profile of v1, /device:TPU:0, one launch (start us, length us, event | category | flops | bytes accessed | tf_op | source)
XLA Modules:
  0.0 671.6 jit_solution(6933437767765731355)
XLA Ops:
  34.7 4.0 fusion.70
  44.0 5.6 collective-permute-done.1
  61.7 12.5 %collective-permute-done.6 = f32[48,768]{1,0:T(8,128)} collective-permute-done((f32[48,768]{1,0:T(8,128)S(1)}, f32[48,768]{1,0:T(8,128)}, u32[]{:S(2)}, u32[]{:S(2)}) %collective-permute-start.6) | collective-permute-done | bytes 147488 | tf_op jit(solution)/shard_map/ppermute | solution.py:24
  85.9 6.9 %collective-permute-done.14 = f32[192,768]{1,0:T(8,128)S(1)} collective-permute-done((f32[192,768]{1,0:T(8,128)}, f32[192,768]{1,0:T(8,128)S(1)}, u32[]{:S(2)}, u32[]{:S(2)}) %collective-permute-start.14) | collective-permute-done | bytes 589856 | tf_op jit(solution)/shard_map/ppermute | solution.py:24
  104.1 11.9 %collective-permute-done.11 = f32[192,1536]{1,0:T(8,128)} collective-permute-done((f32[192,1536]{1,0:T(8,128)}, f32[192,1536]{1,0:T(8,128)}, u32[]{:S(2)}, u32[]{:S(2)}) %collective-permute-start.11) | collective-permute-done | bytes 1179680 | tf_op jit(solution)/shard_map/ppermute | solution.py:24
  127.2 3.4 reshape.439
  140.0 4.1 fusion.71
  154.7 12.2 %multiply_convert_fusion.3 = (bf16[576,1536]{1,0:T(8,128)(2,1)S(1)}, f32[576,1536]{1,0:T(8,128)}, f32[576,1536]{1,0:T(8,128)}) fusion(f32[1536]{0:T(1024)S(1)} %copy-done.98, bf16[768,1536]{1,0:T(8,128)(2,1)} %param.39, f32[576,768]{1,0:T(8,128)S(1)} %get-tuple-element.146, f32[768]{0:T(1024)S(1)} %copy-done.103, f32[768]{0:T(1024)S(1)} %copy-done.96, ...), kind=kOutput, calls=%fused_computation.46 | convolution fusion | flops 1419558912 | bytes 12993024 | tf_op jit(solution)/shard_map/dot_general | solution.py:259
  171.1 11.0 %multiply_convert_fusion.2 = (bf16[576,1536]{1,0:T(8,128)(2,1)S(1)}, f32[576,1536]{1,0:T(8,128)}, f32[576,1536]{1,0:T(8,128)}) fusion(f32[1536]{0:T(1024)S(1)} %slice.436, bf16[768,1536]{1,0:T(8,128)(2,1)S(1)} %shard_map.361, f32[576,768]{1,0:T(8,128)S(1)} %get-tuple-element.146, f32[768]{0:T(1024)S(1)} %copy-done.103, f32[768]{0:T(1024)S(1)} %copy-done.96, ...), kind=kOutput, calls=%fused_computation.33 | convolution fusion | flops 1419558912 | bytes 12993024 | tf_op jit(solution)/shard_map/dot_general | solution.py:259
  182.2 3.2 shard_map.362
  210.2 3.1 fusion.56
  213.5 4.0 convert_bitcast_fusion.1
  219.1 6.9 %convert_reduce_fusion.1 = (f32[1536]{0:T(1024)S(1)}, bf16[576,1536]{1,0:T(8,128)(2,1)S(1)}) fusion(f32[576,1536]{1,0:T(8,128)} %get-tuple-element.107, f32[576,1536]{1,0:T(8,128)} %get-tuple-element.147, bf16[1536,768]{1,0:T(8,128)(2,1)} %param.41, f32[576,768]{1,0:T(8,128)} %get-tuple-element.94), kind=kOutput, calls=%fused_computation.30 | convolution fusion | flops 1373551104 | bytes 12982272 | tf_op jit(solution)/shard_map/dot_general | solution.py:321
  246.7 4.7 fusion.117
  251.4 4.6 convert_reduce_fusion.4
  262.7 4.6 fusion.119
  267.3 4.5 convert_reduce_fusion.2
  271.8 10.9 %convert_reduce_fusion.3 = (f32[6,64]{1,0:T(8,128)S(1)}, bf16[2,288,6,64]{1,3,2,0:T(8,128)(2,1)}) fusion(bf16[2,288,6,64]{1,3,2,0:T(8,128)(2,1)} %copy-done.69, f32[2,6,288,288]{2,3,1,0:T(8,128)} %fusion.119, f32[2,6,288,288]{2,3,1,0:T(8,128)} %copy-done.10, f32[2,6,288]{2,1,0:T(8,128)S(1)} %log_add_fusion), kind=kOutput, calls=%fused_computation.137 | convolution fusion | flops 137026848 | bytes 8862720 | tf_op jit(solution)/shard_map/bhqk,bkhd->bqhd/dot_general | solution.py:191
  282.7 10.6 %fusion.80 = bf16[2,288,6,64]{1,3,2,0:T(8,128)(2,1)} fusion(f32[2,6,288,288]{2,3,1,0:T(8,128)} %fusion.119, f32[2,6,288,288]{2,3,1,0:T(8,128)} %copy-done.10, f32[2,6,288]{2,1,0:T(8,128)S(1)} %log_add_fusion, f32[2,288,6,64]{1,3,2,0:T(8,128)S(1)} %copy-done.40, f32[6,64]{1,0:T(8,128)S(1)} %add.423), kind=kOutput, calls=%fused_computation.130 | convolution fusion | flops 137027232 | bytes 9305088 | tf_op jit(solution)/shard_map/bhqk,bqhd->bkhd/dot_general | solution.py:192
  293.3 10.9 %convert_reduce_fusion.5 = (f32[6,64]{1,0:T(8,128)S(1)}, bf16[2,288,6,64]{1,3,2,0:T(8,128)(2,1)}) fusion(bf16[2,288,6,64]{1,3,2,0:T(8,128)(2,1)} %copy-done.68, f32[2,6,288,288]{2,3,1,0:T(8,128)} %fusion.117, f32[2,6,288,288]{2,3,1,0:T(8,128)} %copy-done.9, f32[2,6,288]{2,1,0:T(8,128)S(1)} %log_add_fusion.1), kind=kOutput, calls=%fused_computation.139 | convolution fusion | flops 137026848 | bytes 8862720 | tf_op jit(solution)/shard_map/bhqk,bkhd->bqhd/dot_general | solution.py:191
  304.2 10.7 %fusion.74 = bf16[2,288,6,64]{1,3,2,0:T(8,128)(2,1)} fusion(f32[2,6,288,288]{2,3,1,0:T(8,128)} %fusion.117, f32[2,6,288,288]{2,3,1,0:T(8,128)} %copy-done.9, f32[2,6,288]{2,1,0:T(8,128)S(1)} %log_add_fusion.1, f32[2,288,6,64]{1,3,2,0:T(8,128)S(1)} %copy-done.38, f32[6,64]{1,0:T(8,128)S(1)} %copy-done.92), kind=kOutput, calls=%fused_computation.128 | convolution fusion | flops 137027232 | bytes 9305088 | tf_op jit(solution)/shard_map/bhqk,bqhd->bkhd/dot_general | solution.py:192
  317.0 3.1 fusion.98
  324.6 3.1 fusion.96
  343.5 3.2 fusion.100
  352.7 3.2 fusion.102
  361.8 3.2 fusion.104
  374.8 4.2 fusion.207
  379.0 4.2 fusion.208
  402.9 3.4 add_add_fusion.mine_ref
  406.3 4.1 fusion.210
  410.7 3.9 fusion.209
  435.4 7.0 %collective-permute-done.40 = f32[192,384]{1,0:T(8,128)S(1)} collective-permute-done((f32[192,384]{1,0:T(8,128)S(1)}, f32[192,384]{1,0:T(8,128)S(1)}, u32[]{:S(2)}, u32[]{:S(2)}) %collective-permute-start.40) | collective-permute-done | bytes 294944 | tf_op jit(solution)/shard_map/ppermute | solution.py:24
  444.1 4.3 collective-permute-done.36
  468.8 4.2 slice_add_fusion
  475.3 6.2 fusion.54
  482.6 10.5 %collective-permute-done.31 = f32[192,1152]{1,0:T(8,128)S(1)} collective-permute-done((f32[192,1152]{1,0:T(8,128)}, f32[192,1152]{1,0:T(8,128)S(1)}, u32[]{:S(2)}, u32[]{:S(2)}) %collective-permute-start.31) | collective-permute-done | bytes 884768 | tf_op jit(solution)/shard_map/ppermute | solution.py:24
  495.3 15.6 %collective-permute-done.27 = f32[192,1152]{1,0:T(8,128)S(1)} collective-permute-done((f32[192,1152]{1,0:T(8,128)S(1)}, f32[192,1152]{1,0:T(8,128)S(1)}, u32[]{:S(2)}, u32[]{:S(2)}) %collective-permute-start.27) | collective-permute-done | bytes 884768 | tf_op jit(solution)/shard_map/ppermute | solution.py:24
  518.7 4.6 collective-permute-done.32
  525.7 7.8 %collective-permute-done.28 = f32[96,1152]{1,0:T(8,128)S(1)} collective-permute-done((f32[96,1152]{1,0:T(8,128)S(1)}, f32[96,1152]{1,0:T(8,128)S(1)}, u32[]{:S(2)}, u32[]{:S(2)}) %collective-permute-start.28) | collective-permute-done | bytes 442400 | tf_op jit(solution)/shard_map/ppermute | solution.py:24
  541.9 10.0 %collective-permute-done.33 = f32[48,1152]{1,0:T(8,128)} collective-permute-done((f32[48,1152]{1,0:T(8,128)}, f32[48,1152]{1,0:T(8,128)}, u32[]{:S(2)}, u32[]{:S(2)}) %collective-permute-start.33) | collective-permute-done | bytes 221216 | tf_op jit(solution)/shard_map/ppermute | solution.py:24
  560.2 4.2 shard_map.364
  569.7 25.4 %collective-permute-done.34 = f32[48,1152]{1,0:T(8,128)} collective-permute-done((f32[48,1152]{1,0:T(8,128)}, f32[48,1152]{1,0:T(8,128)}, u32[]{:S(2)}, u32[]{:S(2)}) %collective-permute-start.34) | collective-permute-done | bytes 221216 | tf_op jit(solution)/shard_map/ppermute | solution.py:28
  600.9 3.8 fusion.55
  606.1 4.4 collective-permute-done.45
  612.1 5.9 collective-permute-done.50
  618.5 16.3 %collective-permute-done.56 = f32[192,1536]{1,0:T(8,128)S(1)} collective-permute-done((f32[192,1536]{1,0:T(8,128)S(1)}, f32[192,1536]{1,0:T(8,128)S(1)}, u32[]{:S(2)}, u32[]{:S(2)}) %collective-permute-start.56) | collective-permute-done | bytes 1179680 | tf_op jit(solution)/shard_map/ppermute | solution.py:24
  639.4 17.3 %collective-permute-done.57 = f32[96,1536]{1,0:T(8,128)S(1)} collective-permute-done((f32[96,1536]{1,0:T(8,128)S(1)}, f32[96,1536]{1,0:T(8,128)S(1)}, u32[]{:S(2)}, u32[]{:S(2)}) %collective-permute-start.57) | collective-permute-done | bytes 589856 | tf_op jit(solution)/shard_map/ppermute | solution.py:24
  658.3 12.4 %collective-permute-done.58 = f32[48,1536]{1,0:T(8,128)S(1)} collective-permute-done((f32[48,1536]{1,0:T(8,128)S(1)}, f32[48,1536]{1,0:T(8,128)S(1)}, u32[]{:S(2)}, u32[]{:S(2)}) %collective-permute-start.58) | collective-permute-done | bytes 294944 | tf_op jit(solution)/shard_map/ppermute | solution.py:24
  (626 shorter events, 321.8 us)
Async XLA Ops:
  2.6 36.2 %collective-permute-start = (f32[288,384]{1,0:T(8,128)}, f32[288,384]{1,0:T(8,128)}, u32[]{:S(2)}, u32[]{:S(2)}) collective-permute-start(f32[288,384]{1,0:T(8,128)} %dynamic-slice_convert_fusion.2), channel_id=1, source_target_pairs={{0,1},{1,0},{2,3},{3,2},{4,5},{5,4},{6,7},{7,6},{8,9},{9,8},{10,11... | collective-permute-start | bytes 1327112 | tf_op jit(solution)/shard_map/ppermute | solution.py:28
  7.0 89.3 %collective-permute-start.4 = (f32[2304]{0:T(1024)S(1)}, f32[2304]{0:T(1024)S(1)}, u32[]{:S(2)}, u32[]{:S(2)}) collective-permute-start(f32[2304]{0:T(1024)S(1)} %pad_maximum_fusion.9), channel_id=1, source_target_pairs={{0,1},{1,0},{2,3},{3,2},{4,5},{5,4},{6,7},{7,6},{8,9},{9,8},{10,11... | collective-permute-start | bytes 27656 | tf_op jit(solution)/shard_map/ppermute | solution.py:28
  8.5 46.5 %collective-permute-start.5 = (f32[48,768]{1,0:T(8,128)}, f32[48,768]{1,0:T(8,128)S(1)}, u32[]{:S(2)}, u32[]{:S(2)}) collective-permute-start(f32[48,768]{1,0:T(8,128)} %dynamic-slice_convert_fusion.3), channel_id=1, source_target_pairs={{0,1},{1,0},{2,3},{3,2},{4,5},{5,4},{6,7},{7,6},{8,9},{9,8},{10,11... | collective-permute-start | bytes 442376 | tf_op jit(solution)/shard_map/ppermute | solution.py:28
  12.4 47.7 %collective-permute-start.9 = (f32[96,1536]{1,0:T(8,128)}, f32[96,1536]{1,0:T(8,128)}, u32[]{:S(2)}, u32[]{:S(2)}) collective-permute-start(f32[96,1536]{1,0:T(8,128)} %dynamic-slice_convert_fusion.1), channel_id=1, source_target_pairs={{0,1},{1,0},{2,3},{3,2},{4,5},{5,4},{6,7},{7,6},{8,9},{9,8},{10,11... | collective-permute-start | bytes 1769480 | tf_op jit(solution)/shard_map/ppermute | solution.py:28
  14.2 64.6 %collective-permute-start.13 = (f32[192,768]{1,0:T(8,128)}, f32[192,768]{1,0:T(8,128)}, u32[]{:S(2)}, u32[]{:S(2)}) collective-permute-start(f32[192,768]{1,0:T(8,128)} %dynamic-slice_convert_fusion), channel_id=1, source_target_pairs={{0,1},{1,0},{2,3},{3,2},{4,5},{5,4},{6,7},{7,6},{8,9},{9,8},{10,11... | collective-permute-start | bytes 1769480 | tf_op jit(solution)/shard_map/ppermute | solution.py:28
  38.8 10.8 %collective-permute-start.1 = (f32[288,384]{1,0:T(8,128)}, f32[288,384]{1,0:T(8,128)S(1)}, u32[]{:S(2)}, u32[]{:S(2)}) collective-permute-start(f32[288,384]{1,0:T(8,128)} %collective-permute-done), channel_id=1, source_target_pairs={{0,8},{2,10},{4,12},{6,14},{8,0},{10,2},{12,4},{14,6},{16,24},{18,... | collective-permute-start | bytes 1327112 | tf_op jit(solution)/shard_map/ppermute | solution.py:24
  51.7 29.7 %collective-permute-start.2 = (f32[576,384]{1,0:T(8,128)}, f32[576,384]{1,0:T(8,128)}, u32[]{:S(2)}, u32[]{:S(2)}) collective-permute-start(f32[576,384]{1,0:T(8,128)} %pad_maximum_fusion.6), channel_id=1, source_target_pairs={{0,4},{2,6},{4,0},{6,2},{8,12},{10,14},{12,8},{14,10},{16,20},{18,... | collective-permute-start | bytes 2654216 | tf_op jit(solution)/shard_map/ppermute | solution.py:24
  55.0 19.2 %collective-permute-start.6 = (f32[48,768]{1,0:T(8,128)S(1)}, f32[48,768]{1,0:T(8,128)}, u32[]{:S(2)}, u32[]{:S(2)}) collective-permute-start(f32[48,768]{1,0:T(8,128)S(1)} %collective-permute-done.5), channel_id=1, source_target_pairs={{0,4},{2,6},{4,0},{6,2},{8,12},{10,14},{12,8},{14,10},{16,20},{18,... | collective-permute-start | bytes 442376 | tf_op jit(solution)/shard_map/ppermute | solution.py:24
  60.1 22.6 %collective-permute-start.10 = (f32[96,1536]{1,0:T(8,128)}, f32[96,1536]{1,0:T(8,128)S(1)}, u32[]{:S(2)}, u32[]{:S(2)}) collective-permute-start(f32[96,1536]{1,0:T(8,128)} %collective-permute-done.9), channel_id=1, source_target_pairs={{0,8},{2,10},{4,12},{6,14},{8,0},{10,2},{12,4},{14,6},{16,24},{18,... | collective-permute-start | bytes 1769480 | tf_op jit(solution)/shard_map/ppermute | solution.py:24
  75.2 10.5 %collective-permute-start.7 = (f32[96,768]{1,0:T(8,128)S(1)}, f32[96,768]{1,0:T(8,128)S(1)}, u32[]{:S(2)}, u32[]{:S(2)}) collective-permute-start(f32[96,768]{1,0:T(8,128)S(1)} %pad_maximum_fusion.7), channel_id=1, source_target_pairs={{0,8},{2,10},{4,12},{6,14},{8,0},{10,2},{12,4},{14,6},{16,24},{18,... | collective-permute-start | bytes 884744 | tf_op jit(solution)/shard_map/ppermute | solution.py:24
  78.8 14.0 %collective-permute-start.14 = (f32[192,768]{1,0:T(8,128)}, f32[192,768]{1,0:T(8,128)S(1)}, u32[]{:S(2)}, u32[]{:S(2)}) collective-permute-start(f32[192,768]{1,0:T(8,128)} %collective-permute-done.13), channel_id=1, source_target_pairs={{0,4},{2,6},{4,0},{6,2},{8,12},{10,14},{12,8},{14,10},{16,20},{18,... | collective-permute-start | bytes 1769480 | tf_op jit(solution)/shard_map/ppermute | solution.py:24
  82.6 38.7 %collective-permute-start.3 = (f32[1152,384]{1,0:T(8,128)S(1)}, f32[1152,384]{1,0:T(8,128)}, u32[]{:S(2)}, u32[]{:S(2)}) collective-permute-start(f32[1152,384]{1,0:T(8,128)S(1)} %constant_dynamic-update-slice_fusion.refs_0_), channel_id=1, source_target_pairs={{0,2},{2,0},{4,6},{6,4},{8,10},{10,8},{12,14},{14,12},{16,18},{18,... | collective-permute-start | bytes 5308424 | tf_op jit(solution)/shard_map/ppermute | solution.py:24
  85.1 30.9 %collective-permute-start.11 = (f32[192,1536]{1,0:T(8,128)}, f32[192,1536]{1,0:T(8,128)}, u32[]{:S(2)}, u32[]{:S(2)}) collective-permute-start(f32[192,1536]{1,0:T(8,128)} %pad_maximum_fusion.4), channel_id=1, source_target_pairs={{0,4},{2,6},{4,0},{6,2},{8,12},{10,14},{12,8},{14,10},{16,20},{18,... | collective-permute-start | bytes 3538952 | tf_op jit(solution)/shard_map/ppermute | solution.py:24
  85.7 14.7 %collective-permute-start.8 = (f32[192,768]{1,0:T(8,128)S(1)}, f32[192,768]{1,0:T(8,128)S(1)}, u32[]{:S(2)}, u32[]{:S(2)}) collective-permute-start(f32[192,768]{1,0:T(8,128)S(1)} %constant_dynamic-update-slice_fusion.3.refs_0_), channel_id=1, source_target_pairs={{0,2},{2,0},{4,6},{6,4},{8,10},{10,8},{12,14},{14,12},{16,18},{18,... | collective-permute-start | bytes 1769480 | tf_op jit(solution)/shard_map/ppermute | solution.py:24
  95.8 22.6 %collective-permute-start.15 = (f32[384,768]{1,0:T(8,128)}, f32[384,768]{1,0:T(8,128)}, u32[]{:S(2)}, u32[]{:S(2)}) collective-permute-start(f32[384,768]{1,0:T(8,128)} %pad_maximum_fusion.5), channel_id=1, source_target_pairs={{0,8},{2,10},{4,12},{6,14},{8,0},{10,2},{12,4},{14,6},{16,24},{18,... | collective-permute-start | bytes 3538952 | tf_op jit(solution)/shard_map/ppermute | solution.py:24
  118.4 50.1 %collective-permute-start.12 = (f32[384,1536]{1,0:T(8,128)}, f32[384,1536]{1,0:T(8,128)}, u32[]{:S(2)}, u32[]{:S(2)}) collective-permute-start(f32[384,1536]{1,0:T(8,128)} %constant_dynamic-update-slice_fusion.6.refs_0_), channel_id=1, source_target_pairs={{0,2},{2,0},{4,6},{6,4},{8,10},{10,8},{12,14},{14,12},{16,18},{18,... | collective-permute-start | bytes 7077896 | tf_op jit(solution)/shard_map/ppermute | solution.py:24
  120.8 61.4 %collective-permute-start.16 = (f32[768,768]{1,0:T(8,128)}, f32[768,768]{1,0:T(8,128)}, u32[]{:S(2)}, u32[]{:S(2)}) collective-permute-start(f32[768,768]{1,0:T(8,128)} %constant_dynamic-update-slice_fusion.9.refs_0_), channel_id=1, source_target_pairs={{0,2},{2,0},{4,6},{6,4},{8,10},{10,8},{12,14},{14,12},{16,18},{18,... | collective-permute-start | bytes 7077896 | tf_op jit(solution)/shard_map/ppermute | solution.py:24
  383.5 27.1 %collective-permute-start.19 = (f32[8456]{0:T(1024)S(1)}, f32[8456]{0:T(1024)S(1)}, u32[]{:S(2)}, u32[]{:S(2)}) collective-permute-start(f32[8456]{0:T(1024)S(1)} %concatenate.64), channel_id=1, source_target_pairs={{0,1},{1,0},{2,3},{3,2},{4,5},{5,4},{6,7},{7,6},{8,9},{9,8},{10,11... | collective-permute-start | bytes 101480 | tf_op jit(solution)/shard_map/ppermute | solution.py:28
  394.4 64.6 %collective-permute-start.30 = (f32[384,1152]{1,0:T(8,128)}, f32[384,1152]{1,0:T(8,128)}, u32[]{:S(2)}, u32[]{:S(2)}) collective-permute-start(f32[384,1152]{1,0:T(8,128)} %slice.454), channel_id=1, source_target_pairs={{0,2},{2,0},{4,6},{6,4},{8,10},{10,8},{12,14},{14,12},{16,18},{18,... | collective-permute-start | bytes 5308424 | tf_op jit(solution)/shard_map/ppermute | solution.py:24
  397.3 66.1 %collective-permute-start.26 = (f32[384,1152]{0,1:T(8,128)}, f32[384,1152]{0,1:T(8,128)}, u32[]{:S(2)}, u32[]{:S(2)}) collective-permute-start(f32[384,1152]{0,1:T(8,128)} %slice.446), channel_id=1, source_target_pairs={{0,2},{2,0},{4,6},{6,4},{8,10},{10,8},{12,14},{14,12},{16,18},{18,... | collective-permute-start | bytes 5308424 | tf_op jit(solution)/shard_map/ppermute | solution.py:24
  400.7 30.7 %collective-permute-start.39 = (f32[384,384]{1,0:T(8,128)}, f32[384,384]{1,0:T(8,128)}, u32[]{:S(2)}, u32[]{:S(2)}) collective-permute-start(f32[384,384]{1,0:T(8,128)} %slice.474), channel_id=1, source_target_pairs={{0,2},{2,0},{4,6},{6,4},{8,10},{10,8},{12,14},{14,12},{16,18},{18,... | collective-permute-start | bytes 1769480 | tf_op jit(solution)/shard_map/ppermute | solution.py:24
  417.0 16.1 %collective-permute-start.35 = (f32[384,384]{1,0:T(8,128)S(1)}, f32[384,384]{1,0:T(8,128)S(1)}, u32[]{:S(2)}, u32[]{:S(2)}) collective-permute-start(f32[384,384]{1,0:T(8,128)S(1)} %slice.466), channel_id=1, source_target_pairs={{0,2},{2,0},{4,6},{6,4},{8,10},{10,8},{12,14},{14,12},{16,18},{18,... | collective-permute-start | bytes 1769480 | tf_op jit(solution)/shard_map/ppermute | solution.py:24
  431.3 37.5 %collective-permute-start.54 = (f32[384,1536]{1,0:T(8,128)}, f32[384,1536]{1,0:T(8,128)}, u32[]{:S(2)}, u32[]{:S(2)}) collective-permute-start(f32[384,1536]{1,0:T(8,128)} %slice.502), channel_id=1, source_target_pairs={{0,2},{2,0},{4,6},{6,4},{8,10},{10,8},{12,14},{14,12},{16,18},{18,... | collective-permute-start | bytes 7077896 | tf_op jit(solution)/shard_map/ppermute | solution.py:24
  433.2 15.2 %collective-permute-start.36 = (f32[192,384]{1,0:T(8,128)S(1)}, f32[192,384]{1,0:T(8,128)S(1)}, u32[]{:S(2)}, u32[]{:S(2)}) collective-permute-start(f32[192,384]{1,0:T(8,128)S(1)} %slice.468), channel_id=1, source_target_pairs={{0,8},{2,10},{4,12},{6,14},{8,0},{10,2},{12,4},{14,6},{16,24},{18,... | collective-permute-start | bytes 884744 | tf_op jit(solution)/shard_map/ppermute | solution.py:24
  454.0 19.0 %collective-permute-start.44 = (f32[384,1664]{1,0:T(8,128)}, f32[384,1664]{1,0:T(8,128)}, u32[]{:S(2)}, u32[]{:S(2)}) collective-permute-start(f32[384,1664]{1,0:T(8,128)} %get-tuple-element.117), channel_id=1, source_target_pairs={{0,2},{2,0},{4,6},{6,4},{8,10},{10,8},{12,14},{14,12},{16,18},{18,... | collective-permute-start | bytes 7667720 | tf_op jit(solution)/shard_map/ppermute | solution.py:24
  456.1 17.9 %collective-permute-start.48 = (f32[384,1664]{1,0:T(8,128)}, f32[384,1664]{1,0:T(8,128)}, u32[]{:S(2)}, u32[]{:S(2)}) collective-permute-start(f32[384,1664]{1,0:T(8,128)} %get-tuple-element.118), channel_id=1, source_target_pairs={{0,2},{2,0},{4,6},{6,4},{8,10},{10,8},{12,14},{14,12},{16,18},{18,... | collective-permute-start | bytes 7667720 | tf_op jit(solution)/shard_map/ppermute | solution.py:24
  459.1 95.1 %collective-permute-start.24 = (f32[576,768]{1,0:T(8,128)S(1)}, f32[576,768]{1,0:T(8,128)}, u32[]{:S(2)}, u32[]{:S(2)}) collective-permute-start(f32[576,768]{1,0:T(8,128)S(1)} %multiply_add_fusion.mine_ref), channel_id=1, source_target_pairs={{0,1},{1,0},{2,3},{3,2},{4,5},{5,4},{6,7},{7,6},{8,9},{9,8},{10,11... | collective-permute-start | bytes 5308424 | tf_op jit(solution)/shard_map/ppermute | solution.py:28
  463.4 90.8 %collective-permute-start.25 = (f32[576,768]{1,0:T(8,128)}, f32[576,768]{1,0:T(8,128)}, u32[]{:S(2)}, u32[]{:S(2)}) collective-permute-start(f32[576,768]{1,0:T(8,128)} %add_add_fusion.mine_ref), channel_id=1, source_target_pairs={{0,1},{1,0},{2,3},{3,2},{4,5},{5,4},{6,7},{7,6},{8,9},{9,8},{10,11... | collective-permute-start | bytes 5308424 | tf_op jit(solution)/shard_map/ppermute | solution.py:28
  468.8 24.3 %collective-permute-start.31 = (f32[192,1152]{1,0:T(8,128)}, f32[192,1152]{1,0:T(8,128)S(1)}, u32[]{:S(2)}, u32[]{:S(2)}) collective-permute-start(f32[192,1152]{1,0:T(8,128)} %slice.456), channel_id=1, source_target_pairs={{0,8},{2,10},{4,12},{6,14},{8,0},{10,2},{12,4},{14,6},{16,24},{18,... | collective-permute-start | bytes 2654216 | tf_op jit(solution)/shard_map/ppermute | solution.py:24
  473.0 62.5 %collective-permute-start.38 = (f32[48,384]{1,0:T(8,128)}, f32[48,384]{1,0:T(8,128)}, u32[]{:S(2)}, u32[]{:S(2)}) collective-permute-start(f32[48,384]{1,0:T(8,128)} %slice.472), channel_id=1, source_target_pairs={{0,16},{2,18},{4,20},{6,22},{8,24},{10,26},{12,28},{14,30},{16,0},... | collective-permute-start | bytes 221192 | tf_op jit(solution)/shard_map/ppermute | solution.py:24
  474.0 36.9 %collective-permute-start.27 = (f32[192,1152]{1,0:T(8,128)S(1)}, f32[192,1152]{1,0:T(8,128)S(1)}, u32[]{:S(2)}, u32[]{:S(2)}) collective-permute-start(f32[192,1152]{1,0:T(8,128)S(1)} %copy-done.80), channel_id=1, source_target_pairs={{0,8},{2,10},{4,12},{6,14},{8,0},{10,2},{12,4},{14,6},{16,24},{18,... | collective-permute-start | bytes 2654216 | tf_op jit(solution)/shard_map/ppermute | solution.py:24
  493.1 46.9 %collective-permute-start.43 = (f32[48,384]{1,0:T(8,128)}, f32[48,384]{1,0:T(8,128)S(1)}, u32[]{:S(2)}, u32[]{:S(2)}) collective-permute-start(f32[48,384]{1,0:T(8,128)} %slice_add_fusion.25), channel_id=1, source_target_pairs={{0,1},{1,0},{2,3},{3,2},{4,5},{5,4},{6,7},{7,6},{8,9},{9,8},{10,11... | collective-permute-start | bytes 221192 | tf_op jit(solution)/shard_map/ppermute | solution.py:28
  511.8 11.5 %collective-permute-start.32 = (f32[96,1152]{1,0:T(8,128)}, f32[96,1152]{1,0:T(8,128)}, u32[]{:S(2)}, u32[]{:S(2)}) collective-permute-start(f32[96,1152]{1,0:T(8,128)} %slice.458), channel_id=1, source_target_pairs={{0,4},{2,6},{4,0},{6,2},{8,12},{10,14},{12,8},{14,10},{16,20},{18,... | collective-permute-start | bytes 1327112 | tf_op jit(solution)/shard_map/ppermute | solution.py:24
  534.3 66.7 %collective-permute-start.53 = (f32[384,1536]{1,0:T(8,128)}, f32[384,1536]{1,0:T(8,128)}, u32[]{:S(2)}, u32[]{:S(2)}) collective-permute-start(f32[384,1536]{1,0:T(8,128)} %slice.500), channel_id=1, source_target_pairs={{0,2},{2,0},{4,6},{6,4},{8,10},{10,8},{12,14},{14,12},{16,18},{18,... | collective-permute-start | bytes 7077896 | tf_op jit(solution)/shard_map/ppermute | solution.py:24
  535.5 65.4 %collective-permute-start.55 = (f32[384,1536]{1,0:T(8,128)}, f32[384,1536]{1,0:T(8,128)}, u32[]{:S(2)}, u32[]{:S(2)}) collective-permute-start(f32[384,1536]{1,0:T(8,128)} %slice_add_fusion), channel_id=1, source_target_pairs={{0,1},{1,0},{2,3},{3,2},{4,5},{5,4},{6,7},{7,6},{8,9},{9,8},{10,11... | collective-permute-start | bytes 7077896 | tf_op jit(solution)/shard_map/ppermute | solution.py:28
  540.0 11.9 %collective-permute-start.33 = (f32[48,1152]{1,0:T(8,128)}, f32[48,1152]{1,0:T(8,128)}, u32[]{:S(2)}, u32[]{:S(2)}) collective-permute-start(f32[48,1152]{1,0:T(8,128)} %slice.460), channel_id=1, source_target_pairs={{0,16},{2,18},{4,20},{6,22},{8,24},{10,26},{12,28},{14,30},{16,0},... | collective-permute-start | bytes 663560 | tf_op jit(solution)/shard_map/ppermute | solution.py:24
  551.9 46.9 %collective-permute-start.49 = (f32[192,1664]{1,0:T(8,128)}, f32[192,1664]{1,0:T(8,128)}, u32[]{:S(2)}, u32[]{:S(2)}) collective-permute-start(f32[192,1664]{1,0:T(8,128)} %slice.493), channel_id=1, source_target_pairs={{0,4},{2,6},{4,0},{6,2},{8,12},{10,14},{12,8},{14,10},{16,20},{18,... | collective-permute-start | bytes 3833864 | tf_op jit(solution)/shard_map/ppermute | solution.py:24
  554.2 11.3 %collective-permute-start.29 = (f32[48,1152]{1,0:T(8,128)S(1)}, f32[48,1152]{1,0:T(8,128)S(1)}, u32[]{:S(2)}, u32[]{:S(2)}) collective-permute-start(f32[48,1152]{1,0:T(8,128)S(1)} %copy.347), channel_id=1, source_target_pairs={{0,16},{2,18},{4,20},{6,22},{8,24},{10,26},{12,28},{14,30},{16,0},... | collective-permute-start | bytes 663560 | tf_op jit(solution)/shard_map/ppermute | solution.py:24
  554.2 40.8 %collective-permute-start.34 = (f32[48,1152]{1,0:T(8,128)}, f32[48,1152]{1,0:T(8,128)}, u32[]{:S(2)}, u32[]{:S(2)}) collective-permute-start(f32[48,1152]{1,0:T(8,128)} %slice_add_fusion.22), channel_id=1, source_target_pairs={{0,1},{1,0},{2,3},{3,2},{4,5},{5,4},{6,7},{7,6},{8,9},{9,8},{10,11... | collective-permute-start | bytes 663560 | tf_op jit(solution)/shard_map/ppermute | solution.py:28
  566.2 44.3 %collective-permute-start.45 = (f32[192,1664]{1,0:T(8,128)}, f32[192,1664]{1,0:T(8,128)}, u32[]{:S(2)}, u32[]{:S(2)}) collective-permute-start(f32[192,1664]{1,0:T(8,128)} %slice.485), channel_id=1, source_target_pairs={{0,4},{2,6},{4,0},{6,2},{8,12},{10,14},{12,8},{14,10},{16,20},{18,... | collective-permute-start | bytes 3833864 | tf_op jit(solution)/shard_map/ppermute | solution.py:24
  600.6 17.4 %collective-permute-start.50 = (f32[96,1664]{1,0:T(8,128)S(1)}, f32[96,1664]{1,0:T(8,128)S(1)}, u32[]{:S(2)}, u32[]{:S(2)}) collective-permute-start(f32[96,1664]{1,0:T(8,128)S(1)} %slice.495), channel_id=1, source_target_pairs={{0,8},{2,10},{4,12},{6,14},{8,0},{10,2},{12,4},{14,6},{16,24},{18,... | collective-permute-start | bytes 1916936 | tf_op jit(solution)/shard_map/ppermute | solution.py:24
  604.8 30.0 %collective-permute-start.56 = (f32[192,1536]{1,0:T(8,128)S(1)}, f32[192,1536]{1,0:T(8,128)S(1)}, u32[]{:S(2)}, u32[]{:S(2)}) collective-permute-start(f32[192,1536]{1,0:T(8,128)S(1)} %slice.504), channel_id=1, source_target_pairs={{0,4},{2,6},{4,0},{6,2},{8,12},{10,14},{12,8},{14,10},{16,20},{18,... | collective-permute-start | bytes 3538952 | tf_op jit(solution)/shard_map/ppermute | solution.py:24
  612.0 25.6 %collective-permute-start.46 = (f32[96,1664]{1,0:T(8,128)S(1)}, f32[96,1664]{1,0:T(8,128)S(1)}, u32[]{:S(2)}, u32[]{:S(2)}) collective-permute-start(f32[96,1664]{1,0:T(8,128)S(1)} %slice.487), channel_id=1, source_target_pairs={{0,8},{2,10},{4,12},{6,14},{8,0},{10,2},{12,4},{14,6},{16,24},{18,... | collective-permute-start | bytes 1916936 | tf_op jit(solution)/shard_map/ppermute | solution.py:24
  618.1 19.7 %collective-permute-start.51 = (f32[48,1664]{1,0:T(8,128)S(1)}, f32[48,1664]{1,0:T(8,128)S(1)}, u32[]{:S(2)}, u32[]{:S(2)}) collective-permute-start(f32[48,1664]{1,0:T(8,128)S(1)} %slice.497), channel_id=1, source_target_pairs={{0,16},{2,18},{4,20},{6,22},{8,24},{10,26},{12,28},{14,30},{16,0},... | collective-permute-start | bytes 958472 | tf_op jit(solution)/shard_map/ppermute | solution.py:24
  635.0 21.8 %collective-permute-start.57 = (f32[96,1536]{1,0:T(8,128)S(1)}, f32[96,1536]{1,0:T(8,128)S(1)}, u32[]{:S(2)}, u32[]{:S(2)}) collective-permute-start(f32[96,1536]{1,0:T(8,128)S(1)} %slice.506), channel_id=1, source_target_pairs={{0,8},{2,10},{4,12},{6,14},{8,0},{10,2},{12,4},{14,6},{16,24},{18,... | collective-permute-start | bytes 1769480 | tf_op jit(solution)/shard_map/ppermute | solution.py:24
  637.7 19.2 %collective-permute-start.47 = (f32[48,1664]{1,0:T(8,128)S(1)}, f32[48,1664]{1,0:T(8,128)S(1)}, u32[]{:S(2)}, u32[]{:S(2)}) collective-permute-start(f32[48,1664]{1,0:T(8,128)S(1)} %slice.489), channel_id=1, source_target_pairs={{0,16},{2,18},{4,20},{6,22},{8,24},{10,26},{12,28},{14,30},{16,0},... | collective-permute-start | bytes 958472 | tf_op jit(solution)/shard_map/ppermute | solution.py:24
  637.9 19.1 %collective-permute-start.52 = (f32[48,1664]{1,0:T(8,128)S(1)}, f32[48,1664]{1,0:T(8,128)S(1)}, u32[]{:S(2)}, u32[]{:S(2)}) collective-permute-start(f32[48,1664]{1,0:T(8,128)S(1)} %slice_add_fusion.17), channel_id=1, source_target_pairs={{0,1},{1,0},{2,3},{3,2},{4,5},{5,4},{6,7},{7,6},{8,9},{9,8},{10,11... | collective-permute-start | bytes 958472 | tf_op jit(solution)/shard_map/ppermute | solution.py:28
  656.8 13.9 %collective-permute-start.58 = (f32[48,1536]{1,0:T(8,128)S(1)}, f32[48,1536]{1,0:T(8,128)S(1)}, u32[]{:S(2)}, u32[]{:S(2)}) collective-permute-start(f32[48,1536]{1,0:T(8,128)S(1)} %slice.508), channel_id=1, source_target_pairs={{0,16},{2,18},{4,20},{6,22},{8,24},{10,26},{12,28},{14,30},{16,0},... | collective-permute-start | bytes 884744 | tf_op jit(solution)/shard_map/ppermute | solution.py:24
  (142 other events, 1055.4 us)
